TPU v7x, 1024 devices: a whole 8x8x8 slice. The times are simulated.
1024 devices in a mesh: dp: 8 (over z_lo, core), section: 16 (over z_hi, x), mp: 8 (over y).
Axes of the slice: x: 8, y: 8, z: 8 (z_hi: 2, z_lo: 4; z = z_hi * 4 + z_lo), core: 2. Of those that a mesh axis runs over, the one named last changes fastest.
Arguments:
- tokens: bfloat16 [4, 256, 4608], P(None, 'dp', 'mp'), may hold values from -6 to 6
- gain: float32 [16, 4608], P('section', 'mp'), may hold values from 0.1 to 1.9
- value_weight: bfloat16 [16, 4608, 2048], P('section', 'mp'), may hold values from -0.09375 to 0.09375
- out_weight: bfloat16 [16, 2048, 4608], P('section', None, 'mp'), may hold values from -0.125 to 0.125
- grad_prev: bfloat16 [8, 16, 1024, 4608], P('dp', 'section', None, 'mp'), may hold values from -18 to 18
- dither: bfloat16 [8, 16, 1024, 4608], P('dp', 'section', None, 'mp'), may hold values from 0 to 255, as said below
Outputs:
- hidden: float32 [16, 4, 256, 4608], P('section', None, 'dp', 'mp')
- grad_sum: bfloat16 [16, 1024, 4608], P('section', 'dp', 'mp')
- grad_scale: float32 [], replicated
Inputs may be any that keep to these rules, and one draw needn't show every extreme that they name: `dither`: whole numbers.
All inputs are finite; a program needn't handle non-finite values. Where the computation divides by a largest or mean magnitude, that divisor is 1e-20 or more.
Results may differ from a plain program's by a relative error of at most 0.04.
Values may be sent and summed in bfloat16 or wider, within the bound.
A program may use at most 32 MiB of HBM per device.

v0:
```python
import jax
import jax.numpy as jnp
from jax import lax
from jax.sharding import PartitionSpec as P


def passed_along(shard, axis, by):
    peers = lax.axis_size(axis)
    pairs = [(i, i + by) for i in range(peers) if 0 <= i + by < peers]
    return lax.ppermute(shard, axis, pairs)


def per_device(tokens, gain, value_weight, out_weight, grad_prev, dither):
    section_index = lax.axis_index("section")
    section_count = lax.axis_size("section")
    micro_count = tokens.shape[0]
    row_count = tokens.shape[1]
    local_width = tokens.shape[2]
    full_width = local_width * lax.axis_size("mp")
    gain_row = gain[0]
    w_value = value_weight[0]
    w_out = out_weight[0]
    value_width = w_value.shape[1]
    grad_local = grad_prev[0, 0]
    levels = dither[0, 0]
    peak_value = lax.pmax(jnp.max(jnp.abs(grad_local)).astype(jnp.float32), ("dp", "section", "mp"))
    factor = 127.0 / peak_value
    shifted = (
        grad_local.astype(jnp.float32) * factor + (levels.astype(jnp.float32) + 0.5) / 256.0 - 0.5
    )
    quantized = lax.optimization_barrier(
        jnp.clip(shifted, -127.0, 127.0).astype(jnp.bfloat16)
    ).astype(jnp.float32)

    def layer(incoming, is_live):

        def project(operand):
            scaled = (operand * gain_row[None, :]).astype(jnp.bfloat16)
            return jnp.dot(scaled, w_value, preferred_element_type=jnp.float32)

        def skipped(operand):
            return jnp.zeros((row_count, value_width), jnp.float32)

        partial_value = lax.cond(is_live, project, skipped, incoming)
        squares = jnp.sum(incoming * incoming, axis=1)
        summed, square_sum = (
            lax.psum(partial_value.astype(jnp.bfloat16), "mp").astype(jnp.float32),
            lax.psum(squares.astype(jnp.bfloat16), "mp").astype(jnp.float32),
        )
        inverse = lax.rsqrt(square_sum / full_width + 1e-06)
        mixed_value = (summed * inverse[:, None]).astype(jnp.bfloat16)

        def finish(operand):
            return operand + jnp.dot(mixed_value, w_out, preferred_element_type=jnp.float32)

        def passed(operand):
            return operand

        return lax.cond(is_live, finish, passed, incoming)

    def advance(turn, state_pair):
        buffer, stored = state_pair
        micro_index = turn - section_index
        first_index = jnp.clip(turn, 0, micro_count - 1)
        first_input = lax.dynamic_index_in_dim(tokens, first_index, 0, keepdims=False).astype(
            jnp.float32
        )
        incoming = jnp.where(section_index == 0, first_input, buffer)
        is_live = jnp.logical_and(micro_index >= 0, micro_index < micro_count)
        result = layer(incoming, is_live)
        slot_index = jnp.clip(micro_index, 0, micro_count - 1)
        current = lax.dynamic_index_in_dim(stored, slot_index, 0, keepdims=False)
        stored = lax.dynamic_update_index_in_dim(
            stored, jnp.where(is_live, result, current), slot_index, 0
        )
        buffer = passed_along(result.astype(jnp.bfloat16), "section", 1).astype(result.dtype)
        return (buffer, stored)

    turn_count = section_count + micro_count - 1
    start_state = (
        jnp.zeros((row_count, local_width), jnp.float32),
        jnp.zeros((micro_count, row_count, local_width), jnp.float32),
    )
    state_pair = lax.fori_loop(0, turn_count, advance, start_state)
    summed_grad = lax.psum_scatter(
        quantized.astype(jnp.bfloat16), "dp", scatter_dimension=0, tiled=True
    )
    stored = state_pair[1]
    return (stored[None], summed_grad[None], peak_value / 127.0)


def solution(mesh):
    placed = (
        P(None, "dp", "mp"),
        P("section", "mp"),
        P("section", "mp", None),
        P("section", None, "mp"),
        P("dp", "section", None, "mp"),
        P("dp", "section", None, "mp"),
    )
    return jax.shard_map(
        per_device,
        mesh=mesh,
        in_specs=placed,
        out_specs=(P("section", None, "dp", "mp"), P("section", "dp", "mp"), P()),
        check_vma=False,
    )
```

profile of v0, /device:TPU:14, one launch (start us, length us, event | category | flops | bytes accessed | tf_op | source)
XLA Modules:
  0.0 1989.0 jit_solution(7106280335058233631)
XLA Ops:
  9.3 126.3 %pmax.7 = f32[]{:T(128)} all-reduce(bf16[]{:T(256)} %abs_reduce_fusion), channel_id=1, replica_groups=mesh['dp'=8,'section'=16,'mp'=8] {'dp','section','mp'}, use_global_device_ids=true, to_apply=%region_10.11 | all-reduce | flops 1 | bytes 6 | tf_op jit(solution)/shard_map/pmax | solution.py:26
  143.8 37.3 %reduce-scatter.4.cloned.1.call-done = bf16[128,576]{1,0:T(8,128)(2,1)} async-done(((bf16[1024,576]{1,0:T(8,128)(2,1)}), bf16[128,576]{1,0:T(8,128)(2,1)}) %reduce-scatter.4.cloned.1.call-update) | async-done | bytes 147472
  182.8 1797.6 %while.17 = (s32[]{:T(128)}, f32[32,576]{1,0:T(8,128)S(1)}, f32[4,32,576]{2,1,0:T(8,128)S(1)}, s32[]{:T(128)}, pred[]{:T(512)}, /*index=5*/bf16[4,32,576]{2,1,0:...) while((s32[]{:T(128)}, f32[32,576]{1,0:T(8,128)S(1)}, ...), condition=%wide.region_8.9_spmd.clone, body=%wide.region_0.8_spmd.clone.sunk | while | flops 151459936 | bytes 7728795 | solution.py:84
  184.5 17.3 psum.29
  201.8 67.3 %all-reduce.2.cloned.1.call-done = bf16[32,2048]{1,0:T(8,128)(2,1)} async-done(((bf16[32,2048]{1,0:T(8,128)(2,1)}), bf16[32,2048]{1,0:T(8,128)(2,1)}) %all-reduce.2.cloned.1.call-update) | async-done | bytes 131088 | tf_op jit(solution)/shard_map/while/body/eval_jaxpr/psum | solution.py:47
  298.5 64.8 %all-reduce.2.cloned.1.call-done = bf16[32,2048]{1,0:T(8,128)(2,1)} async-done(((bf16[32,2048]{1,0:T(8,128)(2,1)}), bf16[32,2048]{1,0:T(8,128)(2,1)}) %all-reduce.2.cloned.1.call-update) | async-done | bytes 131088 | tf_op jit(solution)/shard_map/while/body/eval_jaxpr/psum | solution.py:47
  392.7 64.5 %all-reduce.2.cloned.1.call-done = bf16[32,2048]{1,0:T(8,128)(2,1)} async-done(((bf16[32,2048]{1,0:T(8,128)(2,1)}), bf16[32,2048]{1,0:T(8,128)(2,1)}) %all-reduce.2.cloned.1.call-update) | async-done | bytes 131088 | tf_op jit(solution)/shard_map/while/body/eval_jaxpr/psum | solution.py:47
  486.6 64.5 %all-reduce.2.cloned.1.call-done = bf16[32,2048]{1,0:T(8,128)(2,1)} async-done(((bf16[32,2048]{1,0:T(8,128)(2,1)}), bf16[32,2048]{1,0:T(8,128)(2,1)}) %all-reduce.2.cloned.1.call-update) | async-done | bytes 131088 | tf_op jit(solution)/shard_map/while/body/eval_jaxpr/psum | solution.py:47
  580.4 64.5 %all-reduce.2.cloned.1.call-done = bf16[32,2048]{1,0:T(8,128)(2,1)} async-done(((bf16[32,2048]{1,0:T(8,128)(2,1)}), bf16[32,2048]{1,0:T(8,128)(2,1)}) %all-reduce.2.cloned.1.call-update) | async-done | bytes 131088 | tf_op jit(solution)/shard_map/while/body/eval_jaxpr/psum | solution.py:47
  674.3 64.8 %all-reduce.2.cloned.1.call-done = bf16[32,2048]{1,0:T(8,128)(2,1)} async-done(((bf16[32,2048]{1,0:T(8,128)(2,1)}), bf16[32,2048]{1,0:T(8,128)(2,1)}) %all-reduce.2.cloned.1.call-update) | async-done | bytes 131088 | tf_op jit(solution)/shard_map/while/body/eval_jaxpr/psum | solution.py:47
  768.5 64.8 %all-reduce.2.cloned.1.call-done = bf16[32,2048]{1,0:T(8,128)(2,1)} async-done(((bf16[32,2048]{1,0:T(8,128)(2,1)}), bf16[32,2048]{1,0:T(8,128)(2,1)}) %all-reduce.2.cloned.1.call-update) | async-done | bytes 131088 | tf_op jit(solution)/shard_map/while/body/eval_jaxpr/psum | solution.py:47
  864.9 62.6 %all-reduce.2.cloned.1.call-done = bf16[32,2048]{1,0:T(8,128)(2,1)} async-done(((bf16[32,2048]{1,0:T(8,128)(2,1)}), bf16[32,2048]{1,0:T(8,128)(2,1)}) %all-reduce.2.cloned.1.call-update) | async-done | bytes 131088 | tf_op jit(solution)/shard_map/while/body/eval_jaxpr/psum | solution.py:47
  959.1 62.8 %all-reduce.2.cloned.1.call-done = bf16[32,2048]{1,0:T(8,128)(2,1)} async-done(((bf16[32,2048]{1,0:T(8,128)(2,1)}), bf16[32,2048]{1,0:T(8,128)(2,1)}) %all-reduce.2.cloned.1.call-update) | async-done | bytes 131088 | tf_op jit(solution)/shard_map/while/body/eval_jaxpr/psum | solution.py:47
  1054.1 62.8 %all-reduce.2.cloned.1.call-done = bf16[32,2048]{1,0:T(8,128)(2,1)} async-done(((bf16[32,2048]{1,0:T(8,128)(2,1)}), bf16[32,2048]{1,0:T(8,128)(2,1)}) %all-reduce.2.cloned.1.call-update) | async-done | bytes 131088 | tf_op jit(solution)/shard_map/while/body/eval_jaxpr/psum | solution.py:47
  1149.1 62.8 %all-reduce.2.cloned.1.call-done = bf16[32,2048]{1,0:T(8,128)(2,1)} async-done(((bf16[32,2048]{1,0:T(8,128)(2,1)}), bf16[32,2048]{1,0:T(8,128)(2,1)}) %all-reduce.2.cloned.1.call-update) | async-done | bytes 131088 | tf_op jit(solution)/shard_map/while/body/eval_jaxpr/psum | solution.py:47
  1241.9 65.0 %all-reduce.2.cloned.1.call-done = bf16[32,2048]{1,0:T(8,128)(2,1)} async-done(((bf16[32,2048]{1,0:T(8,128)(2,1)}), bf16[32,2048]{1,0:T(8,128)(2,1)}) %all-reduce.2.cloned.1.call-update) | async-done | bytes 131088 | tf_op jit(solution)/shard_map/while/body/eval_jaxpr/psum | solution.py:47
  1320.5 16.3 psum.29
  1336.8 64.5 %all-reduce.2.cloned.1.call-done = bf16[32,2048]{1,0:T(8,128)(2,1)} async-done(((bf16[32,2048]{1,0:T(8,128)(2,1)}), bf16[32,2048]{1,0:T(8,128)(2,1)}) %all-reduce.2.cloned.1.call-update) | async-done | bytes 131088 | tf_op jit(solution)/shard_map/while/body/eval_jaxpr/psum | solution.py:47
  1430.8 65.6 %all-reduce.2.cloned.1.call-done = bf16[32,2048]{1,0:T(8,128)(2,1)} async-done(((bf16[32,2048]{1,0:T(8,128)(2,1)}), bf16[32,2048]{1,0:T(8,128)(2,1)}) %all-reduce.2.cloned.1.call-update) | async-done | bytes 131088 | tf_op jit(solution)/shard_map/while/body/eval_jaxpr/psum | solution.py:47
  1525.8 65.6 %all-reduce.2.cloned.1.call-done = bf16[32,2048]{1,0:T(8,128)(2,1)} async-done(((bf16[32,2048]{1,0:T(8,128)(2,1)}), bf16[32,2048]{1,0:T(8,128)(2,1)}) %all-reduce.2.cloned.1.call-update) | async-done | bytes 131088 | tf_op jit(solution)/shard_map/while/body/eval_jaxpr/psum | solution.py:47
  1620.8 65.7 %all-reduce.2.cloned.1.call-done = bf16[32,2048]{1,0:T(8,128)(2,1)} async-done(((bf16[32,2048]{1,0:T(8,128)(2,1)}), bf16[32,2048]{1,0:T(8,128)(2,1)}) %all-reduce.2.cloned.1.call-update) | async-done | bytes 131088 | tf_op jit(solution)/shard_map/while/body/eval_jaxpr/psum | solution.py:47
  1715.9 65.0 %all-reduce.2.cloned.1.call-done = bf16[32,2048]{1,0:T(8,128)(2,1)} async-done(((bf16[32,2048]{1,0:T(8,128)(2,1)}), bf16[32,2048]{1,0:T(8,128)(2,1)}) %all-reduce.2.cloned.1.call-update) | async-done | bytes 131088 | tf_op jit(solution)/shard_map/while/body/eval_jaxpr/psum | solution.py:47
  1810.3 64.8 %all-reduce.2.cloned.1.call-done = bf16[32,2048]{1,0:T(8,128)(2,1)} async-done(((bf16[32,2048]{1,0:T(8,128)(2,1)}), bf16[32,2048]{1,0:T(8,128)(2,1)}) %all-reduce.2.cloned.1.call-update) | async-done | bytes 131088 | tf_op jit(solution)/shard_map/while/body/eval_jaxpr/psum | solution.py:47
  1904.5 64.5 %all-reduce.2.cloned.1.call-done = bf16[32,2048]{1,0:T(8,128)(2,1)} async-done(((bf16[32,2048]{1,0:T(8,128)(2,1)}), bf16[32,2048]{1,0:T(8,128)(2,1)}) %all-reduce.2.cloned.1.call-update) | async-done | bytes 131088 | tf_op jit(solution)/shard_map/while/body/eval_jaxpr/psum | solution.py:47
  (342 shorter events, 557.9 us)
Async XLA Ops:
  7.2 173.9 %reduce-scatter.4.cloned.1.call-start = ((), (), s32[]{:S(2)}) async-start(), calls=%async_computation.1 | async-start | bytes 1474560
  182.8 86.3 %all-reduce.2.cloned.1.call-start = ((), (), s32[]{:S(2)}) async-start(), calls=%async_computation.2 | async-start | bytes 262144 | tf_op jit(solution)/shard_map/while/body/eval_jaxpr/psum | solution.py:47
  280.4 82.8 %all-reduce.2.cloned.1.call-start = ((), (), s32[]{:S(2)}) async-start(), calls=%async_computation.2 | async-start | bytes 262144 | tf_op jit(solution)/shard_map/while/body/eval_jaxpr/psum | solution.py:47
  374.6 82.5 %all-reduce.2.cloned.1.call-start = ((), (), s32[]{:S(2)}) async-start(), calls=%async_computation.2 | async-start | bytes 262144 | tf_op jit(solution)/shard_map/while/body/eval_jaxpr/psum | solution.py:47
  468.5 82.5 %all-reduce.2.cloned.1.call-start = ((), (), s32[]{:S(2)}) async-start(), calls=%async_computation.2 | async-start | bytes 262144 | tf_op jit(solution)/shard_map/while/body/eval_jaxpr/psum | solution.py:47
  562.4 82.5 %all-reduce.2.cloned.1.call-start = ((), (), s32[]{:S(2)}) async-start(), calls=%async_computation.2 | async-start | bytes 262144 | tf_op jit(solution)/shard_map/while/body/eval_jaxpr/psum | solution.py:47
  656.3 82.8 %all-reduce.2.cloned.1.call-start = ((), (), s32[]{:S(2)}) async-start(), calls=%async_computation.2 | async-start | bytes 262144 | tf_op jit(solution)/shard_map/while/body/eval_jaxpr/psum | solution.py:47
  750.5 82.8 %all-reduce.2.cloned.1.call-start = ((), (), s32[]{:S(2)}) async-start(), calls=%async_computation.2 | async-start | bytes 262144 | tf_op jit(solution)/shard_map/while/body/eval_jaxpr/psum | solution.py:47
  844.7 82.8 %all-reduce.2.cloned.1.call-start = ((), (), s32[]{:S(2)}) async-start(), calls=%async_computation.2 | async-start | bytes 262144 | tf_op jit(solution)/shard_map/while/body/eval_jaxpr/psum | solution.py:47
  938.9 83.1 %all-reduce.2.cloned.1.call-start = ((), (), s32[]{:S(2)}) async-start(), calls=%async_computation.2 | async-start | bytes 262144 | tf_op jit(solution)/shard_map/while/body/eval_jaxpr/psum | solution.py:47
  1023.5 10.4 collective-permute-start
  1033.9 83.1 %all-reduce.2.cloned.1.call-start = ((), (), s32[]{:S(2)}) async-start(), calls=%async_computation.2 | async-start | bytes 262144 | tf_op jit(solution)/shard_map/while/body/eval_jaxpr/psum | solution.py:47
  1128.8 83.1 %all-reduce.2.cloned.1.call-start = ((), (), s32[]{:S(2)}) async-start(), calls=%async_computation.2 | async-start | bytes 262144 | tf_op jit(solution)/shard_map/while/body/eval_jaxpr/psum | solution.py:47
  1213.5 10.4 collective-permute-start
  1223.8 83.1 %all-reduce.2.cloned.1.call-start = ((), (), s32[]{:S(2)}) async-start(), calls=%async_computation.2 | async-start | bytes 262144 | tf_op jit(solution)/shard_map/while/body/eval_jaxpr/psum | solution.py:47
  1307.9 10.9 collective-permute-start
  1318.8 82.6 %all-reduce.2.cloned.1.call-start = ((), (), s32[]{:S(2)}) async-start(), calls=%async_computation.2 | async-start | bytes 262144 | tf_op jit(solution)/shard_map/while/body/eval_jaxpr/psum | solution.py:47
  1412.8 83.6 %all-reduce.2.cloned.1.call-start = ((), (), s32[]{:S(2)}) async-start(), calls=%async_computation.2 | async-start | bytes 262144 | tf_op jit(solution)/shard_map/while/body/eval_jaxpr/psum | solution.py:47
  1507.8 83.6 %all-reduce.2.cloned.1.call-start = ((), (), s32[]{:S(2)}) async-start(), calls=%async_computation.2 | async-start | bytes 262144 | tf_op jit(solution)/shard_map/while/body/eval_jaxpr/psum | solution.py:47
  1602.8 83.7 %all-reduce.2.cloned.1.call-start = ((), (), s32[]{:S(2)}) async-start(), calls=%async_computation.2 | async-start | bytes 262144 | tf_op jit(solution)/shard_map/while/body/eval_jaxpr/psum | solution.py:47
  1687.5 10.4 collective-permute-start
  1697.9 83.0 %all-reduce.2.cloned.1.call-start = ((), (), s32[]{:S(2)}) async-start(), calls=%async_computation.2 | async-start | bytes 262144 | tf_op jit(solution)/shard_map/while/body/eval_jaxpr/psum | solution.py:47
  1792.3 82.8 %all-reduce.2.cloned.1.call-start = ((), (), s32[]{:S(2)}) async-start(), calls=%async_computation.2 | async-start | bytes 262144 | tf_op jit(solution)/shard_map/while/body/eval_jaxpr/psum | solution.py:47
  1886.5 82.5 %all-reduce.2.cloned.1.call-start = ((), (), s32[]{:S(2)}) async-start(), calls=%async_computation.2 | async-start | bytes 262144 | tf_op jit(solution)/shard_map/while/body/eval_jaxpr/psum | solution.py:47
  (36 other events, 210.9 us)
Sparse Core Ops, SparseCore 0:
  140.1 40.8 reduce-scatter.3
  186.5 82.5 all-reduce.1
  284.1 79.0 all-reduce.1
  378.0 79.0 all-reduce.1
  471.9 79.0 all-reduce.1
  565.8 79.0 all-reduce.1
  660.0 79.0 all-reduce.1
  754.2 79.0 all-reduce.1
  848.7 78.7 all-reduce.1
  942.9 79.0 all-reduce.1
  1037.9 79.0 all-reduce.1
  1132.8 79.0 all-reduce.1
  1227.5 79.3 all-reduce.1
  1322.2 79.1 all-reduce.1
  1416.2 80.1 all-reduce.1
  1511.2 80.1 all-reduce.1
  1606.2 80.2 all-reduce.1
  1701.3 79.5 all-reduce.1
  1796.0 79.0 all-reduce.1
  1889.9 79.0 all-reduce.1
where the time goes:
time: 1990 us
  waiting for transfers between devices  1300 us (65%)
  blocking collectives  437 us (22%)
  starting transfers between devices  166 us (8%)
  other arithmetic  41.2 us (2%)
    psum x19, waiting for transfers between devices, layer(): lax.psum(partial_value.astype(jnp.bfloat16), 'mp').astype(jnp.float32)  1230 us
    psum x19, blocking collectives, layer(): lax.psum(squares.astype(jnp.bfloat16), 'mp').astype(jnp.float32)  311 us
    ppermute x19, starting transfers between devices, passed_along(): return lax.ppermute(shard, axis, pairs)  165 us
    pmax x1, blocking collectives, per_device(): lax.pmax(jnp.max(jnp.abs(grad_local)).astype(jnp.float32), ('dp', 'sectio...  126 us
  transfers between devices with their start and end apart: 39, of which 39 were waited for; matrix products, arithmetic and copies ran while one was open for 0% of the time, Pallas kernels for 0%

commit v1 on v0

v1 whole, which is shorter than its diff:
```python
import functools

import jax
import jax.numpy as jnp
from jax import lax
from jax.experimental import pallas as pl
from jax.experimental.pallas import tpu as pltpu
from jax.sharding import PartitionSpec as P

MESH = pl.DeviceIdType.MESH
BF16, F32 = jnp.bfloat16, jnp.float32
CHUNK = 16
LAG_SUM = 2
LAG_OUT = 4


def wait_bytes(ref, sem):
    pltpu.make_async_copy(ref, ref, sem).wait()


def kernel(sizes, tokens, gain, w_value_hbm, w_out_hbm, grad_hbm, dither_hbm,
           hidden_out, sum_out, scale_out,
           w_value, w_own, w_prev, grad, levels,
           here, before, hidden, partial, parts, square, squares, value, gathered, gathered_own,
           quant, quants, peaks, peaks_dp, peaks_mp, peaks_sec,
           load_sem, part_s, part_r, square_s, square_r, value_s, value_r, own_r,
           ahead_s, before_r, back_s, hidden_r, ship_s, ship_r, twin_s, twin_r,
           quant_s, quant_r, peak_s, peak_r):
    n_dp, n_sec, n_mp = sizes
    chunks, rows, width = here.shape
    value_width = partial.shape[2]
    block = value_width // n_mp
    per_micro = tokens.shape[1] // rows
    half = w_prev.shape[0] // 2
    share = quant.shape[1]
    dp, sec, mp = (lax.axis_index(a) for a in ("dp", "section", "mp"))
    twin = dp + 1 - 2 * lax.rem(dp, 2)

    finishing = (0, n_sec // 2 - 1, n_sec - 1)

    def is_in(index, members):
        found = index == members[0]
        for member in members[1:]:
            found = jnp.logical_or(found, index == member)
        return found

    finishes = is_in(sec, finishing)
    hands_on = jnp.logical_not(finishes)
    takes_value = jnp.logical_and(sec > 0, jnp.logical_not(is_in(sec - 1, finishing)))
    takes_hidden = jnp.logical_and(sec > 0, is_in(sec - 1, finishing))
    first = sec == 0
    late = sec >= n_sec // 2

    def load(i, src, dst):
        return pltpu.make_async_copy(src, dst, load_sem.at[i])

    loads = [
        load(0, w_value_hbm.at[0], w_value),
        load(1, w_out_hbm.at[0], w_own),
        load(2, grad_hbm.at[0, 0], grad),
        load(3, dither_hbm.at[0, 0], levels),
    ]
    for item in loads:
        item.start()

    barrier = pltpu.get_barrier_semaphore()

    def greet(**where):
        pl.semaphore_signal(barrier, inc=1, device_id=where, device_id_type=MESH)

    for r in range(1, n_dp):
        greet(dp=lax.rem(dp + r, n_dp))
    for r in range(1, n_mp):
        greet(mp=lax.rem(mp + r, n_mp))
    for r in range(1, n_sec):
        greet(section=lax.rem(sec + r, n_sec))

    @pl.when(sec < n_sec - 1)
    def _():
        for r in range(1, n_mp):
            greet(section=sec + 1, mp=lax.rem(mp + r, n_mp))

    @pl.when(sec > 0)
    def _():
        for r in range(1, n_mp):
            greet(section=sec - 1, mp=lax.rem(mp + r, n_mp))

    sides = (sec > 0).astype(jnp.int32) + (sec < n_sec - 1).astype(jnp.int32)
    pl.semaphore_wait(barrier, n_dp + n_sec + n_mp - 3 + (n_mp - 1) * sides)

    def remote(src, dst, send, recv, **where):
        return pltpu.make_async_remote_copy(src, dst, send, recv, device_id=where, device_id_type=MESH)

    mine = pl.ds(pl.multiple_of(lax.rem(dp, 2) * half, half), half)
    other = pl.ds(pl.multiple_of(lax.rem(twin, 2) * half, half), half)

    @pl.when(hands_on)
    def _():
        remote(w_out_hbm.at[0, mine], w_prev.at[mine], ship_s, ship_r, section=sec + 1).start()

    def local_peak():
        loads[2].wait()

        def step(i, best):
            piece = grad[pl.ds(pl.multiple_of(i * 32, 32), 32), :].astype(F32)
            return jnp.maximum(best, jnp.abs(piece))

        best = lax.fori_loop(0, grad.shape[0] // 32, step, jnp.zeros((32, width), F32))
        best = jnp.max(jnp.max(best, axis=1, keepdims=True), axis=0, keepdims=True)
        peaks[0] = jnp.broadcast_to(best, (1, 128))

    def send_peak(stage, axis, size, index, dst):
        for r in range(1, size):
            remote(peaks.at[stage], dst.at[r - 1], peak_s.at[stage], peak_r.at[stage],
                   **{axis: lax.rem(index + r, size)}).start()

    def take_peak(stage, dst):
        wait_bytes(dst, peak_r.at[stage])
        peaks[stage + 1] = jnp.maximum(peaks[stage], jnp.max(dst[...], axis=0))

    def peak_a():
        local_peak()
        send_peak(0, "dp", n_dp, dp, peaks_dp)

    def peak_b():
        take_peak(0, peaks_dp)
        send_peak(1, "mp", n_mp, mp, peaks_mp)

    def peak_c():
        take_peak(1, peaks_mp)
        send_peak(2, "section", n_sec, sec, peaks_sec)

    def gradient():
        take_peak(2, peaks_sec)
        peak = peaks[3][:, :1]
        scale_out[...] = jnp.broadcast_to(peak / 127.0, scale_out.shape)
        factor = 127.0 / peak
        loads[3].wait()
        per = share // 32

        def step(i, carry):
            at = pl.ds(pl.multiple_of(i * 32, 32), 32)
            shifted = grad[at, :].astype(F32) * factor + (levels[at, :].astype(F32) + 0.5) / 256.0 - 0.5
            into = pl.ds(pl.multiple_of(lax.rem(i, per) * 32, 32), 32)
            quant[i // per, into, :] = jnp.clip(shifted, -127.0, 127.0).astype(BF16)
            return carry

        lax.fori_loop(0, n_dp * per, step, 0)
        for r in range(n_dp - 1, 0, -1):
            to = lax.rem(dp + r, n_dp)
            remote(quant.at[to], quants.at[r - 1], quant_s, quant_r, dp=to).start()
        wait_bytes(quants, quant_r)

        def add(i, carry):
            at = pl.ds(pl.multiple_of(i * 16, 16), 16)
            total = quant[dp, at, :].astype(F32)
            for r in range(n_dp - 1):
                total = total + quants[r, at, :].astype(F32)
            sum_out[0, at, :] = total.astype(BF16)
            return carry

        lax.fori_loop(0, share // 16, add, 0)

    @pl.when(jnp.logical_not(first))
    def _():
        peak_a()
        peak_b()
        peak_c()

    @pl.when(takes_value)
    def _():
        wait_bytes(w_prev.at[mine], ship_r)
        remote(w_prev.at[mine], w_prev.at[mine], twin_s, twin_r, dp=twin).start()

    @pl.when(late)
    def _():
        gradient()

    loads[0].wait()
    loads[1].wait()

    @pl.when(takes_value)
    def _():
        wait_bytes(w_prev.at[other], twin_r)

    diagonal = (lax.broadcasted_iota(jnp.int32, (rows, 128), 0)
                == lax.broadcasted_iota(jnp.int32, (rows, 128), 1))
    full_width = width * n_mp

    def project(c):
        @pl.when(first)
        def _():
            at = pl.ds(pl.multiple_of(lax.rem(c, per_micro) * rows, rows), rows)
            here[c] = tokens[c // per_micro, at, :].astype(F32)

        @pl.when(takes_hidden)
        def _():
            wait_bytes(before.at[c], before_r.at[c])
            here[c] = before[c]

        @pl.when(takes_value)
        def _():
            wait_bytes(before.at[c], before_r.at[c])
            wait_bytes(gathered.at[c], value_r.at[c])
            here[c] = before[c] + jnp.dot(gathered[c], w_prev[...], preferred_element_type=F32)

        state = here[c]
        summed = jnp.sum(state * state, axis=1, keepdims=True)
        square[c] = jnp.sum(jnp.where(diagonal, summed, 0.0), axis=0, keepdims=True)
        for r in (4, 3, 5, 2, 6, 1, 7):
            if r < n_mp:
                remote(square.at[c], squares.at[c, r - 1], square_s.at[c], square_r.at[c],
                       mp=lax.rem(mp + r, n_mp)).start()
        scaled = (state * gain[...]).astype(BF16)
        partial[c] = jnp.dot(scaled, w_value[...], preferred_element_type=F32).astype(BF16)
        for r in (4, 3, 5, 2, 6, 1, 7):
            if r < n_mp:
                to = lax.rem(mp + r, n_mp)
                columns = pl.ds(pl.multiple_of(to * block, block), block)
                remote(partial.at[c, :, columns], parts.at[c, r - 1], part_s.at[c], part_r.at[c], mp=to).start()

        @pl.when(hands_on)
        def _():
            remote(here.at[c], before.at[c], ahead_s.at[c], before_r.at[c], section=sec + 1).start()

        @pl.when(takes_value)
        def _():
            remote(here.at[c], hidden.at[c], back_s.at[c], hidden_r.at[c], section=sec - 1).start()

    def normalise(c):
        wait_bytes(squares.at[c], square_r.at[c])
        total_square = square[c]
        for r in range(n_mp - 1):
            total_square = total_square + squares[c, r]
        column = jnp.sum(jnp.where(diagonal, total_square, 0.0), axis=1, keepdims=True)
        inverse = lax.rsqrt(column / full_width + 1e-06)
        wait_bytes(parts.at[c], part_r.at[c])
        columns = pl.ds(pl.multiple_of(mp * block, block), block)
        total = partial[c, :, columns].astype(F32)
        for r in range(n_mp - 1):
            total = total + parts[c, r].astype(F32)
        value[c] = (total * inverse).astype(BF16)

        @pl.when(finishes)
        def _():
            for r in (4, 3, 5, 2, 6, 1, 7):
                if r < n_mp:
                    remote(value.at[c], gathered_own.at[c, :, columns], value_s.at[c], own_r.at[c],
                           mp=lax.rem(mp + r, n_mp)).start()
            pltpu.make_async_copy(value.at[c], gathered_own.at[c, :, columns], own_r.at[c]).start()

        @pl.when(hands_on)
        def _():
            for r in (4, 3, 5, 2, 6, 1, 7, 0):
                if r < n_mp:
                    remote(value.at[c], gathered.at[c, :, columns], value_s.at[c], value_r.at[c],
                           section=sec + 1, mp=lax.rem(mp + r, n_mp)).start()

    def finish(c):
        wait_bytes(gathered_own.at[c], own_r.at[c])
        hidden[c] = here[c] + jnp.dot(gathered_own[c], w_own[...], preferred_element_type=F32)

        @pl.when(sec < n_sec - 1)
        def _():
            remote(hidden.at[c], before.at[c], ahead_s.at[c], before_r.at[c], section=sec + 1).start()

    def within(c):
        return jnp.logical_and(c >= 0, c < chunks)

    def turn(i, carry):
        @pl.when(within(i))
        def _():
            project(i)

        @pl.when(jnp.logical_and(finishes, within(i - LAG_OUT)))
        def _():
            finish(i - LAG_OUT)

        @pl.when(within(i - LAG_SUM))
        def _():
            normalise(i - LAG_SUM)

        for k, stage in ((2, peak_a), (3, peak_b), (5, peak_c)):
            @pl.when(jnp.logical_and(first, i == k))
            def _(stage=stage):
                stage()

        return carry

    lax.fori_loop(0, chunks + LAG_OUT, turn, 0)

    @pl.when(jnp.logical_not(late))
    def _():
        gradient()

    def close(c, carry):
        wait_bytes(squares.at[c], square_s.at[c])
        wait_bytes(parts.at[c], part_s.at[c])

        @pl.when(finishes)
        def _():
            wait_bytes(gathered_own.at[c, :, pl.ds(0, value_width - block)], value_s.at[c])

        @pl.when(hands_on)
        def _():
            wait_bytes(gathered_own.at[c], value_s.at[c])
            wait_bytes(hidden.at[c], hidden_r.at[c])

        @pl.when(sec < n_sec - 1)
        def _():
            wait_bytes(here.at[c], ahead_s.at[c])

        @pl.when(takes_value)
        def _():
            wait_bytes(here.at[c], back_s.at[c])

        at = pl.ds(pl.multiple_of(lax.rem(c, per_micro) * rows, rows), rows)
        hidden_out[0, c // per_micro, at, :] = hidden[c]
        return carry

    lax.fori_loop(0, chunks, close, 0)
    wait_bytes(quants, quant_s)
    wait_bytes(peaks_dp, peak_s.at[0])
    wait_bytes(peaks_mp, peak_s.at[1])
    wait_bytes(peaks_sec, peak_s.at[2])

    @pl.when(hands_on)
    def _():
        wait_bytes(w_prev.at[mine], ship_s)

    @pl.when(takes_value)
    def _():
        wait_bytes(w_prev.at[mine], twin_s)


def solution(mesh):
    n_dp, n_sec, n_mp = (mesh.shape[a] for a in ("dp", "section", "mp"))

    def per_device(tokens, gain, w_value, w_out, grad_prev, dither):
        micro, batch, width = tokens.shape
        value_width = w_value.shape[2]
        grad_rows = grad_prev.shape[2]
        rows = CHUNK
        chunks = micro * batch // rows
        block = value_width // n_mp
        share = grad_rows // n_dp
        vmem, hbm = pl.BlockSpec(memory_space=pltpu.VMEM), pl.BlockSpec(memory_space=pl.ANY)
        dma = pltpu.SemaphoreType.DMA
        state = pltpu.VMEM((chunks, rows, width), F32)
        wide = pltpu.VMEM((chunks, rows, value_width), BF16)
        hidden, summed, scale = pl.pallas_call(
            functools.partial(kernel, (n_dp, n_sec, n_mp)),
            out_shape=(
                jax.ShapeDtypeStruct((1, micro, batch, width), F32),
                jax.ShapeDtypeStruct((1, share, width), BF16),
                jax.ShapeDtypeStruct((8, 128), F32),
            ),
            in_specs=[vmem, vmem, hbm, hbm, hbm, hbm],
            out_specs=(vmem, vmem, vmem),
            scratch_shapes=[
                pltpu.VMEM((width, value_width), BF16),
                pltpu.VMEM((value_width, width), BF16),
                pltpu.VMEM((value_width, width), BF16),
                pltpu.VMEM((grad_rows, width), BF16),
                pltpu.VMEM((grad_rows, width), BF16),
                state, state, state,
                wide,
                pltpu.VMEM((chunks, n_mp - 1, rows, block), BF16),
                pltpu.VMEM((chunks, 1, 128), F32),
                pltpu.VMEM((chunks, n_mp - 1, 1, 128), F32),
                pltpu.VMEM((chunks, rows, block), BF16),
                wide, wide,
                pltpu.VMEM((n_dp, share, width), BF16),
                pltpu.VMEM((n_dp - 1, share, width), BF16),
                pltpu.VMEM((4, 1, 128), F32),
                pltpu.VMEM((n_dp - 1, 1, 128), F32),
                pltpu.VMEM((n_mp - 1, 1, 128), F32),
                pltpu.VMEM((n_sec - 1, 1, 128), F32),
                dma((4,)),
                dma((chunks,)), dma((chunks,)), dma((chunks,)), dma((chunks,)),
                dma((chunks,)), dma((chunks,)), dma((chunks,)),
                dma((chunks,)), dma((chunks,)), dma((chunks,)), dma((chunks,)),
                dma, dma, dma, dma, dma, dma,
                dma((3,)), dma((3,)),
            ],
            compiler_params=pltpu.CompilerParams(
                collective_id=0, has_side_effects=True, vmem_limit_bytes=48 * 1024 * 1024
            ),
        )(tokens, gain, w_value, w_out, grad_prev, dither)
        return hidden, summed, scale[0, 0]

    return jax.shard_map(
        per_device,
        mesh=mesh,
        in_specs=(
            P(None, "dp", "mp"),
            P("section", "mp"),
            P("section", "mp", None),
            P("section", None, "mp"),
            P("dp", "section", None, "mp"),
            P("dp", "section", None, "mp"),
        ),
        out_specs=(P("section", None, "dp", "mp"), P("section", "dp", "mp"), P()),
        check_vma=False,
    )
```

time: 1990 us -> 288 us (0.14)
  the two profiles are of different devices: /device:TPU:14 before, /device:TPU:782 now
where the time goes in v1:
time: 288 us
  Pallas kernels  276 us (96%)
  local copies, waits for them, and re-layouts  11.4 us (4%)
    pallas_call x1, Pallas kernels, per_device(): pl.pallas_call(functools.partial(kernel, (n_dp, n_sec, n_mp)), out_shape=...  276 us
    unnamed x11, local copies, waits for them, and re-layouts  10.9 us

profile of v1, /device:TPU:782, one launch (start us, length us, event | category | flops | bytes accessed | tf_op | source)
XLA Modules:
  0.0 287.7 jit_solution(696598990999673730)
XLA Ops:
  0.6 1.7 copy.10.grad_hbm
  2.3 1.7 copy.11.dither_hbm
  4.0 0.0 copy-start.1
  4.0 0.0 copy-start.2
  4.0 4.4 %copy.9.w_out_hbm = bf16[1,2048,576]{2,1,0:T(8,128)(2,1)} copy(bf16[1,2048,576]{1,2,0:T(8,128)(2,1)} %param.9) | data formatting | bytes 4718592 | tf_op args[3]
  8.4 0.0 copy-done.1
  8.4 0.0 copy-done.2
  8.4 0.0 copy-start
  8.4 1.7 copy-done
  10.1 275.6 %shard_map.85 = (f32[1,4,32,576]{3,2,1,0:T(8,128)S(1)}, bf16[1,128,576]{2,1,0:T(8,128)(2,1)S(1)}, f32[8,128]{1,0:T(8,128)S(1)}) custom-call(bf16[4,32,576]{2,1,0:T(8,128)(2,1)S(1)} %copy-done.1, f32[1,576]{1,0:T(1,128)S(1)} %copy-done.2, bf16[1,576,2048]{2,1,0:T(8,128)(2,1)S(1)} %copy-done, bf16[1,2048,576]{2,1,0:T(8,128)(2,1)} %copy.9.w_out_hbm, ...), custom_call_target="tpu_custom_call" | custom-call | tf_op jit(solution)/shard_map/pallas_call | solution.py:351
  285.7 0.5 slice.3
  286.2 0.8 copy.12
  287.0 0.7 copy.14
Async XLA Ops:
  4.0 4.4 %copy-start.1 = (bf16[4,32,576]{2,1,0:T(8,128)(2,1)S(1)}, bf16[4,32,576]{2,1,0:T(8,128)(2,1)}, u32[]{:S(2)}) copy-start(bf16[4,32,576]{2,1,0:T(8,128)(2,1)} %tokens.1) | copy-start | bytes 442372
  4.0 4.4 %copy-start.2 = (f32[1,576]{1,0:T(1,128)S(1)}, f32[1,576]{1,0:T(1,128)}, u32[]{:S(2)}) copy-start(f32[1,576]{1,0:T(1,128)} %gain.1) | copy-start | bytes 6916
  8.4 1.7 copy-start

commit v2 on v1

--- a/solution.py
+++ b/solution.py
@@ -10,8 +10,12 @@
 MESH = pl.DeviceIdType.MESH
 BF16, F32 = jnp.bfloat16, jnp.float32
 CHUNK = 16
-LAG_SUM = 2
-LAG_OUT = 4
+LAG_SUM = 1
+LAG_OUT = 2
+
+
+def far_first(n):
+    return sorted(range(n), key=lambda r: (-min(r, n - r), r))
 
 
 def wait_bytes(ref, sem):
@@ -22,7 +26,7 @@
            hidden_out, sum_out, scale_out,
            w_value, w_own, w_prev, grad, levels,
            here, before, hidden, partial, parts, square, squares, value, gathered, gathered_own,
-           quant, quants, peaks, peaks_dp, peaks_mp, peaks_sec,
+           quant, quants, peaks, peaks_dp, peaks_mp, peaks_sec, peaks_opposite,
            load_sem, part_s, part_r, square_s, square_r, value_s, value_r, own_r,
            ahead_s, before_r, back_s, hidden_r, ship_s, ship_r, twin_s, twin_r,
            quant_s, quant_r, peak_s, peak_r):
@@ -35,8 +39,12 @@
     share = quant.shape[1]
     dp, sec, mp = (lax.axis_index(a) for a in ("dp", "section", "mp"))
     twin = dp + 1 - 2 * lax.rem(dp, 2)
-
-    finishing = (0, n_sec // 2 - 1, n_sec - 1)
+    ring = n_sec // 2
+    place = lax.rem(sec, ring)
+    base = sec - place
+    opposite = lax.rem(sec + ring, n_sec)
+
+    finishing = (0, 1, n_sec // 2 - 1, n_sec - 1)
 
     def is_in(index, members):
         found = index == members[0]
@@ -49,19 +57,30 @@
     takes_value = jnp.logical_and(sec > 0, jnp.logical_not(is_in(sec - 1, finishing)))
     takes_hidden = jnp.logical_and(sec > 0, is_in(sec - 1, finishing))
     first = sec == 0
-    late = sec >= n_sec // 2
+    late = sec >= n_sec * 5 // 8
+
+    out_order = far_first(n_mp)
+    in_order = out_order[::-1]
+
+    def block_at(i):
+        return pl.ds(pl.multiple_of(i * block, block), block)
+
+    def slot_of(origin):
+        r = lax.rem(mp + n_mp - origin, n_mp)
+        slot = 0
+        for i, distance in enumerate(in_order):
+            slot = jnp.where(r == distance, i, slot)
+        return slot
 
     def load(i, src, dst):
         return pltpu.make_async_copy(src, dst, load_sem.at[i])
 
-    loads = [
-        load(0, w_value_hbm.at[0], w_value),
-        load(1, w_out_hbm.at[0], w_own),
-        load(2, grad_hbm.at[0, 0], grad),
-        load(3, dither_hbm.at[0, 0], levels),
-    ]
-    for item in loads:
-        item.start()
+    for i, r in enumerate(out_order):
+        load(0, w_value_hbm.at[0, :, block_at(lax.rem(mp + r, n_mp))], w_value.at[:, block_at(i)]).start()
+    for i, r in enumerate(in_order):
+        load(1, w_out_hbm.at[0, block_at(lax.rem(mp + n_mp - r, n_mp))], w_own.at[block_at(i)]).start()
+    load(2, grad_hbm.at[0, 0], grad).start()
+    load(3, dither_hbm.at[0, 0], levels).start()
 
     barrier = pltpu.get_barrier_semaphore()
 
@@ -72,34 +91,47 @@
         greet(dp=lax.rem(dp + r, n_dp))
     for r in range(1, n_mp):
         greet(mp=lax.rem(mp + r, n_mp))
-    for r in range(1, n_sec):
-        greet(section=lax.rem(sec + r, n_sec))
-
-    @pl.when(sec < n_sec - 1)
+    for r in range(1, ring):
+        greet(section=base + lax.rem(place + r, ring))
+    greet(section=opposite)
+
+    @pl.when(hands_on)
     def _():
         for r in range(1, n_mp):
             greet(section=sec + 1, mp=lax.rem(mp + r, n_mp))
 
-    @pl.when(sec > 0)
+    @pl.when(takes_value)
     def _():
         for r in range(1, n_mp):
             greet(section=sec - 1, mp=lax.rem(mp + r, n_mp))
 
-    sides = (sec > 0).astype(jnp.int32) + (sec < n_sec - 1).astype(jnp.int32)
-    pl.semaphore_wait(barrier, n_dp + n_sec + n_mp - 3 + (n_mp - 1) * sides)
+    @pl.when(sec == ring - 1)
+    def _():
+        greet(section=sec + 1)
+
+    @pl.when(sec == ring)
+    def _():
+        greet(section=sec - 1)
+
+    sides = hands_on.astype(jnp.int32) + takes_value.astype(jnp.int32)
+    middle = jnp.logical_or(sec == ring - 1, sec == ring).astype(jnp.int32)
+    pl.semaphore_wait(barrier, n_dp + n_mp + ring - 2 + (n_mp - 1) * sides + middle)
 
     def remote(src, dst, send, recv, **where):
         return pltpu.make_async_remote_copy(src, dst, send, recv, device_id=where, device_id_type=MESH)
 
-    mine = pl.ds(pl.multiple_of(lax.rem(dp, 2) * half, half), half)
-    other = pl.ds(pl.multiple_of(lax.rem(twin, 2) * half, half), half)
+    half_blocks = n_mp // 2
+    a_half = w_prev.at[pl.ds(0, half)]
 
     @pl.when(hands_on)
     def _():
-        remote(w_out_hbm.at[0, mine], w_prev.at[mine], ship_s, ship_r, section=sec + 1).start()
+        for i in range(half_blocks):
+            origin = lax.rem(dp, 2) * half_blocks + i
+            remote(w_out_hbm.at[0, block_at(origin)], w_prev.at[block_at(slot_of(origin))], ship_s, ship_r,
+                   section=sec + 1).start()
 
     def local_peak():
-        loads[2].wait()
+        wait_bytes(grad, load_sem.at[2])
 
         def step(i, best):
             piece = grad[pl.ds(pl.multiple_of(i * 32, 32), 32), :].astype(F32)
@@ -109,10 +141,9 @@
         best = jnp.max(jnp.max(best, axis=1, keepdims=True), axis=0, keepdims=True)
         peaks[0] = jnp.broadcast_to(best, (1, 128))
 
-    def send_peak(stage, axis, size, index, dst):
-        for r in range(1, size):
-            remote(peaks.at[stage], dst.at[r - 1], peak_s.at[stage], peak_r.at[stage],
-                   **{axis: lax.rem(index + r, size)}).start()
+    def send_peak(stage, dst, others):
+        for i, where in enumerate(others):
+            remote(peaks.at[stage], dst.at[i], peak_s.at[stage], peak_r.at[stage], **where).start()
 
     def take_peak(stage, dst):
         wait_bytes(dst, peak_r.at[stage])
@@ -120,22 +151,26 @@
 
     def peak_a():
         local_peak()
-        send_peak(0, "dp", n_dp, dp, peaks_dp)
+        send_peak(0, peaks_dp, [dict(dp=lax.rem(dp + r, n_dp)) for r in range(1, n_dp)])
 
     def peak_b():
         take_peak(0, peaks_dp)
-        send_peak(1, "mp", n_mp, mp, peaks_mp)
+        send_peak(1, peaks_mp, [dict(mp=lax.rem(mp + r, n_mp)) for r in range(1, n_mp)])
 
     def peak_c():
         take_peak(1, peaks_mp)
-        send_peak(2, "section", n_sec, sec, peaks_sec)
+        send_peak(2, peaks_opposite, [dict(section=opposite)])
+
+    def peak_d():
+        take_peak(2, peaks_opposite)
+        send_peak(3, peaks_sec, [dict(section=base + lax.rem(place + r, ring)) for r in range(1, ring)])
 
     def gradient():
-        take_peak(2, peaks_sec)
-        peak = peaks[3][:, :1]
+        take_peak(3, peaks_sec)
+        peak = peaks[4][:, :1]
         scale_out[...] = jnp.broadcast_to(peak / 127.0, scale_out.shape)
         factor = 127.0 / peak
-        loads[3].wait()
+        wait_bytes(levels, load_sem.at[3])
         per = share // 32
 
         def step(i, carry):
@@ -166,27 +201,37 @@
         peak_a()
         peak_b()
         peak_c()
+        peak_d()
 
     @pl.when(takes_value)
     def _():
-        wait_bytes(w_prev.at[mine], ship_r)
-        remote(w_prev.at[mine], w_prev.at[mine], twin_s, twin_r, dp=twin).start()
+        wait_bytes(a_half, ship_r)
+        for i in range(half_blocks):
+            at = block_at(slot_of(lax.rem(dp, 2) * half_blocks + i))
+            remote(w_prev.at[at], w_prev.at[at], twin_s, twin_r, dp=twin).start()
 
     @pl.when(late)
     def _():
         gradient()
 
-    loads[0].wait()
-    loads[1].wait()
+    wait_bytes(w_value, load_sem.at[0])
+    wait_bytes(w_own, load_sem.at[1])
 
     @pl.when(takes_value)
     def _():
-        wait_bytes(w_prev.at[other], twin_r)
+        wait_bytes(a_half, twin_r)
 
     diagonal = (lax.broadcasted_iota(jnp.int32, (rows, 128), 0)
                 == lax.broadcasted_iota(jnp.int32, (rows, 128), 1))
     full_width = width * n_mp
 
+    near = (n_mp // 2 + 1) * block
+
+    def mixed(c, blocks, sems, weight):
+        wait_bytes(blocks.at[c, :, pl.ds(0, near)], sems.at[c, 0])
+        wait_bytes(blocks.at[c, :, pl.ds(near, value_width - near)], sems.at[c, 1])
+        return jnp.dot(blocks[c], weight[...], preferred_element_type=F32)
+
     def project(c):
         @pl.when(first)
         def _():
@@ -201,23 +246,21 @@
         @pl.when(takes_value)
         def _():
             wait_bytes(before.at[c], before_r.at[c])
-            wait_bytes(gathered.at[c], value_r.at[c])
-            here[c] = before[c] + jnp.dot(gathered[c], w_prev[...], preferred_element_type=F32)
+            here[c] = before[c] + mixed(c, gathered, value_r, w_prev)
 
         state = here[c]
         summed = jnp.sum(state * state, axis=1, keepdims=True)
         square[c] = jnp.sum(jnp.where(diagonal, summed, 0.0), axis=0, keepdims=True)
-        for r in (4, 3, 5, 2, 6, 1, 7):
-            if r < n_mp:
-                remote(square.at[c], squares.at[c, r - 1], square_s.at[c], square_r.at[c],
-                       mp=lax.rem(mp + r, n_mp)).start()
         scaled = (state * gain[...]).astype(BF16)
-        partial[c] = jnp.dot(scaled, w_value[...], preferred_element_type=F32).astype(BF16)
-        for r in (4, 3, 5, 2, 6, 1, 7):
-            if r < n_mp:
-                to = lax.rem(mp + r, n_mp)
-                columns = pl.ds(pl.multiple_of(to * block, block), block)
-                remote(partial.at[c, :, columns], parts.at[c, r - 1], part_s.at[c], part_r.at[c], mp=to).start()
+        middle = value_width // 2
+        for start in (0, middle):
+            product = jnp.dot(scaled, w_value[:, start:start + middle], preferred_element_type=F32)
+            partial[c, :, start:start + middle] = product.astype(BF16)
+            for i, r in enumerate(out_order):
+                if r > 0 and start <= i * block < start + middle:
+                    to = lax.rem(mp + r, n_mp)
+                    remote(partial.at[c, :, block_at(i)], parts.at[c, r - 1], part_s.at[c], part_r.at[c], mp=to).start()
+                    remote(square.at[c], squares.at[c, r - 1], square_s.at[c], square_r.at[c], mp=to).start()
 
         @pl.when(hands_on)
         def _():
@@ -235,30 +278,32 @@
         column = jnp.sum(jnp.where(diagonal, total_square, 0.0), axis=1, keepdims=True)
         inverse = lax.rsqrt(column / full_width + 1e-06)
         wait_bytes(parts.at[c], part_r.at[c])
-        columns = pl.ds(pl.multiple_of(mp * block, block), block)
-        total = partial[c, :, columns].astype(F32)
+        total = partial[c, :, value_width - block:].astype(F32)
         for r in range(n_mp - 1):
             total = total + parts[c, r].astype(F32)
         value[c] = (total * inverse).astype(BF16)
 
+        def into(blocks, r):
+            return blocks.at[c, :, block_at(in_order.index(r))]
+
+        def group(r):
+            return 0 if in_order.index(r) * block < near else 1
+
         @pl.when(finishes)
         def _():
-            for r in (4, 3, 5, 2, 6, 1, 7):
-                if r < n_mp:
-                    remote(value.at[c], gathered_own.at[c, :, columns], value_s.at[c], own_r.at[c],
-                           mp=lax.rem(mp + r, n_mp)).start()
-            pltpu.make_async_copy(value.at[c], gathered_own.at[c, :, columns], own_r.at[c]).start()
+            for r in out_order[:-1]:
+                remote(value.at[c], into(gathered_own, r), value_s.at[c], own_r.at[c, group(r)],
+                       mp=lax.rem(mp + r, n_mp)).start()
+            pltpu.make_async_copy(value.at[c], into(gathered_own, 0), own_r.at[c, 0]).start()
 
         @pl.when(hands_on)
         def _():
-            for r in (4, 3, 5, 2, 6, 1, 7, 0):
-                if r < n_mp:
-                    remote(value.at[c], gathered.at[c, :, columns], value_s.at[c], value_r.at[c],
-                           section=sec + 1, mp=lax.rem(mp + r, n_mp)).start()
+            for r in out_order:
+                remote(value.at[c], into(gathered, r), value_s.at[c], value_r.at[c, group(r)],
+                       section=sec + 1, mp=lax.rem(mp + r, n_mp)).start()
 
     def finish(c):
-        wait_bytes(gathered_own.at[c], own_r.at[c])
-        hidden[c] = here[c] + jnp.dot(gathered_own[c], w_own[...], preferred_element_type=F32)
+        hidden[c] = here[c] + mixed(c, gathered_own, own_r, w_own)
 
         @pl.when(sec < n_sec - 1)
         def _():
@@ -272,22 +317,24 @@
         def _():
             project(i)
 
+        @pl.when(within(i - LAG_SUM))
+        def _():
+            normalise(i - LAG_SUM)
+
         @pl.when(jnp.logical_and(finishes, within(i - LAG_OUT)))
         def _():
             finish(i - LAG_OUT)
 
-        @pl.when(within(i - LAG_SUM))
-        def _():
-            normalise(i - LAG_SUM)
-
-        for k, stage in ((2, peak_a), (3, peak_b), (5, peak_c)):
-            @pl.when(jnp.logical_and(first, i == k))
-            def _(stage=stage):
-                stage()
-
         return carry
 
     lax.fori_loop(0, chunks + LAG_OUT, turn, 0)
+
+    @pl.when(first)
+    def _():
+        peak_a()
+        peak_b()
+        peak_c()
+        peak_d()
 
     @pl.when(jnp.logical_not(late))
     def _():
@@ -322,15 +369,16 @@
     wait_bytes(quants, quant_s)
     wait_bytes(peaks_dp, peak_s.at[0])
     wait_bytes(peaks_mp, peak_s.at[1])
-    wait_bytes(peaks_sec, peak_s.at[2])
+    wait_bytes(peaks_opposite, peak_s.at[2])
+    wait_bytes(peaks_sec, peak_s.at[3])
 
     @pl.when(hands_on)
     def _():
-        wait_bytes(w_prev.at[mine], ship_s)
+        wait_bytes(a_half, ship_s)
 
     @pl.when(takes_value)
     def _():
-        wait_bytes(w_prev.at[mine], twin_s)
+        wait_bytes(a_half, twin_s)
 
 
 def solution(mesh):
@@ -372,16 +420,17 @@
                 wide, wide,
                 pltpu.VMEM((n_dp, share, width), BF16),
                 pltpu.VMEM((n_dp - 1, share, width), BF16),
-                pltpu.VMEM((4, 1, 128), F32),
+                pltpu.VMEM((5, 1, 128), F32),
                 pltpu.VMEM((n_dp - 1, 1, 128), F32),
                 pltpu.VMEM((n_mp - 1, 1, 128), F32),
-                pltpu.VMEM((n_sec - 1, 1, 128), F32),
+                pltpu.VMEM((n_sec // 2 - 1, 1, 128), F32),
+                pltpu.VMEM((1, 1, 128), F32),
                 dma((4,)),
                 dma((chunks,)), dma((chunks,)), dma((chunks,)), dma((chunks,)),
-                dma((chunks,)), dma((chunks,)), dma((chunks,)),
+                dma((chunks,)), dma((chunks, 2)), dma((chunks, 2)),
                 dma((chunks,)), dma((chunks,)), dma((chunks,)), dma((chunks,)),
                 dma, dma, dma, dma, dma, dma,
-                dma((3,)), dma((3,)),
+                dma((4,)), dma((4,)),
             ],
             compiler_params=pltpu.CompilerParams(
                 collective_id=0, has_side_effects=True, vmem_limit_bytes=48 * 1024 * 1024

time: 288 us -> 245 us (0.85)
  the two profiles are of different devices: /device:TPU:782 before, /device:TPU:526 now
where the time goes in v2:
time: 245 us; the launch traced here: 244 us
  Pallas kernels  232 us (95%)
  local copies, waits for them, and re-layouts  11.4 us (5%)
    pallas_call x1, Pallas kernels, per_device(): pl.pallas_call(functools.partial(kernel, (n_dp, n_sec, n_mp)), out_shape=...  232 us
    unnamed x11, local copies, waits for them, and re-layouts  10.9 us

profile of v2, /device:TPU:526, one launch (start us, length us, event | category | flops | bytes accessed | tf_op | source)
XLA Modules:
  0.0 244.2 jit_solution(17799296104386245585)
XLA Ops:
  0.6 1.7 copy.10.grad_hbm
  2.3 1.7 copy.11.dither_hbm
  4.0 0.0 copy-start.1
  4.0 0.0 copy-start.2
  4.0 4.4 %copy.9.w_out_hbm = bf16[1,2048,576]{2,1,0:T(8,128)(2,1)} copy(bf16[1,2048,576]{1,2,0:T(8,128)(2,1)} %param.9) | data formatting | bytes 4718592 | tf_op args[3]
  8.4 0.0 copy-done.1
  8.4 0.0 copy-done.2
  8.4 0.0 copy-start
  8.4 1.7 copy-done
  10.1 232.1 %shard_map.85 = (f32[1,4,32,576]{3,2,1,0:T(8,128)S(1)}, bf16[1,128,576]{2,1,0:T(8,128)(2,1)S(1)}, f32[8,128]{1,0:T(8,128)S(1)}) custom-call(bf16[4,32,576]{2,1,0:T(8,128)(2,1)S(1)} %copy-done.1, f32[1,576]{1,0:T(1,128)S(1)} %copy-done.2, bf16[1,576,2048]{2,1,0:T(8,128)(2,1)S(1)} %copy-done, bf16[1,2048,576]{2,1,0:T(8,128)(2,1)} %copy.9.w_out_hbm, ...), custom_call_target="tpu_custom_call" | custom-call | tf_op jit(solution)/shard_map/pallas_call | solution.py:399
  242.2 0.5 slice.3
  242.7 0.8 copy.12
  243.5 0.7 copy.14
Async XLA Ops:
  4.0 4.4 %copy-start.1 = (bf16[4,32,576]{2,1,0:T(8,128)(2,1)S(1)}, bf16[4,32,576]{2,1,0:T(8,128)(2,1)}, u32[]{:S(2)}) copy-start(bf16[4,32,576]{2,1,0:T(8,128)(2,1)} %tokens.1) | copy-start | bytes 442372
  4.0 4.4 %copy-start.2 = (f32[1,576]{1,0:T(1,128)S(1)}, f32[1,576]{1,0:T(1,128)}, u32[]{:S(2)}) copy-start(f32[1,576]{1,0:T(1,128)} %gain.1) | copy-start | bytes 6916
  8.4 1.7 copy-start

commit v3 on v2

--- a/solution.py
+++ b/solution.py
@@ -24,7 +24,7 @@
 
 def kernel(sizes, tokens, gain, w_value_hbm, w_out_hbm, grad_hbm, dither_hbm,
            hidden_out, sum_out, scale_out,
-           w_value, w_own, w_prev, grad, levels,
+           w_value, w_own, w_prev, w_own_t, w_prev_t, grad, levels,
            here, before, hidden, partial, parts, square, squares, value, gathered, gathered_own,
            quant, quants, peaks, peaks_dp, peaks_mp, peaks_sec, peaks_opposite,
            load_sem, part_s, part_r, square_s, square_r, value_s, value_r, own_r,
@@ -35,8 +35,8 @@
     value_width = partial.shape[2]
     block = value_width // n_mp
     per_micro = tokens.shape[1] // rows
-    half = w_prev.shape[0] // 2
-    share = quant.shape[1]
+    half = value_width // 2
+    share = quant.shape[2]
     dp, sec, mp = (lax.axis_index(a) for a in ("dp", "section", "mp"))
     twin = dp + 1 - 2 * lax.rem(dp, 2)
     ring = n_sec // 2
@@ -78,7 +78,7 @@
     for i, r in enumerate(out_order):
         load(0, w_value_hbm.at[0, :, block_at(lax.rem(mp + r, n_mp))], w_value.at[:, block_at(i)]).start()
     for i, r in enumerate(in_order):
-        load(1, w_out_hbm.at[0, block_at(lax.rem(mp + n_mp - r, n_mp))], w_own.at[block_at(i)]).start()
+        load(1, w_out_hbm.at[0, :, block_at(lax.rem(mp + n_mp - r, n_mp))], w_own.at[:, block_at(i)]).start()
     load(2, grad_hbm.at[0, 0], grad).start()
     load(3, dither_hbm.at[0, 0], levels).start()
 
@@ -117,17 +117,21 @@
     middle = jnp.logical_or(sec == ring - 1, sec == ring).astype(jnp.int32)
     pl.semaphore_wait(barrier, n_dp + n_mp + ring - 2 + (n_mp - 1) * sides + middle)
 
+    next_sec = sec + 1
+    ring_mp = [lax.rem(mp + r, n_mp) for r in range(n_mp)]
+
     def remote(src, dst, send, recv, **where):
+        where = {"dp": dp, "section": sec, "mp": mp, **where}
         return pltpu.make_async_remote_copy(src, dst, send, recv, device_id=where, device_id_type=MESH)
 
     half_blocks = n_mp // 2
-    a_half = w_prev.at[pl.ds(0, half)]
+    a_half = w_prev.at[:, pl.ds(0, half)]
 
     @pl.when(hands_on)
     def _():
         for i in range(half_blocks):
             origin = lax.rem(dp, 2) * half_blocks + i
-            remote(w_out_hbm.at[0, block_at(origin)], w_prev.at[block_at(slot_of(origin))], ship_s, ship_r,
+            remote(w_out_hbm.at[0, :, block_at(origin)], w_prev.at[:, block_at(slot_of(origin))], ship_s, ship_r,
                    section=sec + 1).start()
 
     def local_peak():
@@ -137,7 +141,7 @@
             piece = grad[pl.ds(pl.multiple_of(i * 32, 32), 32), :].astype(F32)
             return jnp.maximum(best, jnp.abs(piece))
 
-        best = lax.fori_loop(0, grad.shape[0] // 32, step, jnp.zeros((32, width), F32))
+        best = lax.fori_loop(0, grad.shape[0] // 32, step, jnp.zeros((32, grad.shape[1]), F32))
         best = jnp.max(jnp.max(best, axis=1, keepdims=True), axis=0, keepdims=True)
         peaks[0] = jnp.broadcast_to(best, (1, 128))
 
@@ -171,16 +175,16 @@
         scale_out[...] = jnp.broadcast_to(peak / 127.0, scale_out.shape)
         factor = 127.0 / peak
         wait_bytes(levels, load_sem.at[3])
-        per = share // 32
 
         def step(i, carry):
             at = pl.ds(pl.multiple_of(i * 32, 32), 32)
             shifted = grad[at, :].astype(F32) * factor + (levels[at, :].astype(F32) + 0.5) / 256.0 - 0.5
-            into = pl.ds(pl.multiple_of(lax.rem(i, per) * 32, 32), 32)
-            quant[i // per, into, :] = jnp.clip(shifted, -127.0, 127.0).astype(BF16)
+            rounded = jnp.clip(shifted, -127.0, 127.0).astype(BF16)
+            for j in range(n_dp):
+                quant[j, at, :] = rounded[:, j * share:(j + 1) * share]
             return carry
 
-        lax.fori_loop(0, n_dp * per, step, 0)
+        lax.fori_loop(0, width // 32, step, 0)
         for r in range(n_dp - 1, 0, -1):
             to = lax.rem(dp + r, n_dp)
             remote(quant.at[to], quants.at[r - 1], quant_s, quant_r, dp=to).start()
@@ -194,7 +198,7 @@
             sum_out[0, at, :] = total.astype(BF16)
             return carry
 
-        lax.fori_loop(0, share // 16, add, 0)
+        lax.fori_loop(0, width // 16, add, 0)
 
     @pl.when(jnp.logical_not(first))
     def _():
@@ -208,18 +212,31 @@
         wait_bytes(a_half, ship_r)
         for i in range(half_blocks):
             at = block_at(slot_of(lax.rem(dp, 2) * half_blocks + i))
-            remote(w_prev.at[at], w_prev.at[at], twin_s, twin_r, dp=twin).start()
+            remote(w_prev.at[:, at], w_prev.at[:, at], twin_s, twin_r, dp=twin).start()
 
     @pl.when(late)
     def _():
         gradient()
+
+    def turned(src, dst):
+        def step(i, carry):
+            at = block_at(i)
+            dst[at, :] = src[:, at].T
+            return carry
+
+        lax.fori_loop(0, n_mp, step, 0)
 
     wait_bytes(w_value, load_sem.at[0])
     wait_bytes(w_own, load_sem.at[1])
 
+    @pl.when(jnp.logical_and(finishes, jnp.logical_not(first)))
+    def _():
+        turned(w_own, w_own_t)
+
     @pl.when(takes_value)
     def _():
         wait_bytes(a_half, twin_r)
+        turned(w_prev, w_prev_t)
 
     diagonal = (lax.broadcasted_iota(jnp.int32, (rows, 128), 0)
                 == lax.broadcasted_iota(jnp.int32, (rows, 128), 1))
@@ -227,10 +244,10 @@
 
     near = (n_mp // 2 + 1) * block
 
-    def mixed(c, blocks, sems, weight):
+    def mixed(c, blocks, sems, weight, contracted=0):
         wait_bytes(blocks.at[c, :, pl.ds(0, near)], sems.at[c, 0])
         wait_bytes(blocks.at[c, :, pl.ds(near, value_width - near)], sems.at[c, 1])
-        return jnp.dot(blocks[c], weight[...], preferred_element_type=F32)
+        return lax.dot_general(blocks[c], weight[...], (((1,), (contracted,)), ((), ())), preferred_element_type=F32)
 
     def project(c):
         @pl.when(first)
@@ -246,7 +263,7 @@
         @pl.when(takes_value)
         def _():
             wait_bytes(before.at[c], before_r.at[c])
-            here[c] = before[c] + mixed(c, gathered, value_r, w_prev)
+            here[c] = before[c] + mixed(c, gathered, value_r, w_prev_t)
 
         state = here[c]
         summed = jnp.sum(state * state, axis=1, keepdims=True)
@@ -258,8 +275,9 @@
             partial[c, :, start:start + middle] = product.astype(BF16)
             for i, r in enumerate(out_order):
                 if r > 0 and start <= i * block < start + middle:
-                    to = lax.rem(mp + r, n_mp)
-                    remote(partial.at[c, :, block_at(i)], parts.at[c, r - 1], part_s.at[c], part_r.at[c], mp=to).start()
+                    to = ring_mp[r]
+                    columns = pl.ds(i * block, block)
+                    remote(partial.at[c, :, columns], parts.at[c, r - 1], part_s.at[c], part_r.at[c], mp=to).start()
                     remote(square.at[c], squares.at[c, r - 1], square_s.at[c], square_r.at[c], mp=to).start()
 
         @pl.when(hands_on)
@@ -284,7 +302,7 @@
         value[c] = (total * inverse).astype(BF16)
 
         def into(blocks, r):
-            return blocks.at[c, :, block_at(in_order.index(r))]
+            return blocks.at[c, :, pl.ds(in_order.index(r) * block, block)]
 
         def group(r):
             return 0 if in_order.index(r) * block < near else 1
@@ -293,17 +311,23 @@
         def _():
             for r in out_order[:-1]:
                 remote(value.at[c], into(gathered_own, r), value_s.at[c], own_r.at[c, group(r)],
-                       mp=lax.rem(mp + r, n_mp)).start()
+                       mp=ring_mp[r]).start()
             pltpu.make_async_copy(value.at[c], into(gathered_own, 0), own_r.at[c, 0]).start()
 
         @pl.when(hands_on)
         def _():
             for r in out_order:
                 remote(value.at[c], into(gathered, r), value_s.at[c], value_r.at[c, group(r)],
-                       section=sec + 1, mp=lax.rem(mp + r, n_mp)).start()
+                       section=next_sec, mp=ring_mp[r]).start()
 
     def finish(c):
-        hidden[c] = here[c] + mixed(c, gathered_own, own_r, w_own)
+        @pl.when(first)
+        def _():
+            hidden[c] = here[c] + mixed(c, gathered_own, own_r, w_own, 1)
+
+        @pl.when(jnp.logical_not(first))
+        def _():
+            hidden[c] = here[c] + mixed(c, gathered_own, own_r, w_own_t)
 
         @pl.when(sec < n_sec - 1)
         def _():
@@ -400,17 +424,19 @@
             functools.partial(kernel, (n_dp, n_sec, n_mp)),
             out_shape=(
                 jax.ShapeDtypeStruct((1, micro, batch, width), F32),
-                jax.ShapeDtypeStruct((1, share, width), BF16),
+                jax.ShapeDtypeStruct((1, width, share), BF16),
                 jax.ShapeDtypeStruct((8, 128), F32),
             ),
             in_specs=[vmem, vmem, hbm, hbm, hbm, hbm],
             out_specs=(vmem, vmem, vmem),
             scratch_shapes=[
                 pltpu.VMEM((width, value_width), BF16),
+                pltpu.VMEM((width, value_width), BF16),
+                pltpu.VMEM((width, value_width), BF16),
                 pltpu.VMEM((value_width, width), BF16),
                 pltpu.VMEM((value_width, width), BF16),
-                pltpu.VMEM((grad_rows, width), BF16),
-                pltpu.VMEM((grad_rows, width), BF16),
+                pltpu.VMEM((width, grad_rows), BF16),
+                pltpu.VMEM((width, grad_rows), BF16),
                 state, state, state,
                 wide,
                 pltpu.VMEM((chunks, n_mp - 1, rows, block), BF16),
@@ -418,8 +444,8 @@
                 pltpu.VMEM((chunks, n_mp - 1, 1, 128), F32),
                 pltpu.VMEM((chunks, rows, block), BF16),
                 wide, wide,
-                pltpu.VMEM((n_dp, share, width), BF16),
-                pltpu.VMEM((n_dp - 1, share, width), BF16),
+                pltpu.VMEM((n_dp, width, share), BF16),
+                pltpu.VMEM((n_dp - 1, width, share), BF16),
                 pltpu.VMEM((5, 1, 128), F32),
                 pltpu.VMEM((n_dp - 1, 1, 128), F32),
                 pltpu.VMEM((n_mp - 1, 1, 128), F32),
@@ -433,10 +459,10 @@
                 dma((4,)), dma((4,)),
             ],
             compiler_params=pltpu.CompilerParams(
-                collective_id=0, has_side_effects=True, vmem_limit_bytes=48 * 1024 * 1024
+                collective_id=0, has_side_effects=True, vmem_limit_bytes=60 * 1024 * 1024
             ),
-        )(tokens, gain, w_value, w_out, grad_prev, dither)
-        return hidden, summed, scale[0, 0]
+        )(tokens, gain, w_value, jnp.swapaxes(w_out, 1, 2), jnp.swapaxes(grad_prev, 2, 3), jnp.swapaxes(dither, 2, 3))
+        return hidden, jnp.swapaxes(summed, 1, 2), scale[0, 0]
 
     return jax.shard_map(
         per_device,

time: 245 us -> 240 us (0.980)
  local copies, waits for them, and re-layouts: 11.4 us -> 4.49 us
    unnamed x11 -> x2, local copies, waits for them, and re-layouts: 10.9 us -> 3.3 us
where the time goes in v3:
time: 240 us; the launch traced here: 239 us
  Pallas kernels  234 us (98%)
  local copies, waits for them, and re-layouts  4.49 us (2%)
    pallas_call x1, Pallas kernels, per_device(): pl.pallas_call(functools.partial(kernel, (n_dp, n_sec, n_mp)), out_shape=...  234 us

profile of v3, /device:TPU:526, one launch (start us, length us, event | category | flops | bytes accessed | tf_op | source)
XLA Modules:
  0.0 239.0 jit_solution(11499240972801552556)
XLA Ops:
  0.6 233.9 %shard_map.85 = (f32[1,4,32,576]{3,2,1,0:T(8,128)}, bf16[1,576,128]{2,1,0:T(8,128)(2,1)}, f32[8,128]{1,0:T(8,128)}) custom-call(bf16[4,32,576]{2,1,0:T(8,128)(2,1)} %tokens.1, f32[1,576]{1,0:T(1,128)} %gain.1, bf16[1,576,2048]{2,1,0:T(8,128)(2,1)} %w_value_hbm.1, bf16[1,576,2048]{2,1,0:T(8,128)(2,1)} %bitcast.5, bf16[1,1,576,1024]{3,2,1,0:T(8,128)(2,1)} %bitcast.6, ...), custom_call_target="tpu_custom_call" | custom-call | tf_op jit(solution)/shard_map/pallas_call | solution.py:423
  234.5 1.2 slice.3
  235.7 1.7 copy.11
  237.4 1.6 copy.12
